TPU v7x, 256 devices: a whole 4x4x8 slice. The times are simulated.
256 devices in a mesh: seq: 32 (over x, z), fsdp: 8 (over y, core).
Axes of the slice: x: 4, y: 4, z: 8, core: 2. Of those that a mesh axis runs over, the one named last changes fastest.
Arguments:
- frames: bfloat16 [8, 4096, 1536], P('fsdp', 'seq'), may hold values from -6 to 6
- lengths: int32 [8, 4], P('fsdp'), may hold values from 1 to 2048, 4096 in all within a row
- offsets: int32 [8, 33], P('fsdp'), may hold values from 0 to 4096, as said below
- w_in: bfloat16 [1536, 3072], P('fsdp'), may hold values from -0.15625 to 0.15625
- kernel: float32 [31, 1536], replicated, may hold values from -1 to 1
- cotangent: bfloat16 [8, 8192, 1536], P('fsdp', 'seq'), may hold values from -6 to 6
Outputs:
- owner_output: bfloat16 [8, 8192, 1536], P('fsdp', 'seq')
- frame_grad: bfloat16 [8, 4096, 1536], P('fsdp', 'seq')
- w_grad: float32 [1536, 3072], P(('seq', 'fsdp'))
Inputs may be any that keep to these rules, and one draw needn't show every extreme that they name: Row g: device i of seq owns the frames offsets[g, i] to offsets[g, i + 1] - 1; offsets[g, 0] = 0 and offsets[g, 32] = 4096; each device owns 128 // 4 to 256 frames, beginning within 64 of i * 128; in every group one device owns exactly 256. `lengths`: each row sums to 4096; its largest entry is exactly 2048.
All inputs are finite; a program needn't handle non-finite values.
Results may differ from a plain program's by a relative error of at most 0.025.
Values may be sent and summed in bfloat16 or wider, within the bound.
No kernel may reach another device: no remote copies, remote signals or barrier semaphores. Data moves between devices by JAX's collectives and lax.ppermute only.
A program may use at most 128 MiB of HBM per device.

v0:
```python
import math
import jax
import jax.numpy as jnp
from jax import lax
from jax.sharding import PartitionSpec as P

epsilon = 1e-05


def passed_along(value, axis, steps):
    count = lax.axis_size(axis)
    initial, last = (max(0, -steps), min(count, count - steps))
    return lax.ppermute(value, axis, [(source, source + steps) for source in range(initial, last)])


def normalize_rows(values):
    values = values.astype(jnp.float32)
    center = jnp.mean(values, axis=-1, keepdims=True)
    shifted = values - center
    scale_inv = lax.rsqrt(jnp.mean(shifted * shifted, axis=-1, keepdims=True) + epsilon)
    return (shifted * scale_inv, scale_inv)


def norm_backward(upstream, normed, scale_inv):
    first_mean = jnp.mean(upstream, axis=-1, keepdims=True)
    second_mean = jnp.mean(upstream * normed, axis=-1, keepdims=True)
    return scale_inv * (upstream - first_mean - normed * second_mean)


def depthwise(window, kernel, labels, row_count):
    tap_count = kernel.shape[0]
    half_width = tap_count // 2
    centre = labels[half_width : half_width + row_count]
    result = jnp.zeros((row_count, kernel.shape[1]), jnp.float32)
    for tap_index in range(tap_count):
        same_utt = (labels[tap_index : tap_index + row_count] == centre).astype(jnp.float32)
        result = (
            result
            + kernel[tap_index]
            * window[tap_index : tap_index + row_count].astype(jnp.float32)
            * same_utt[:, None]
        )
    return result


def depthwise_back(window, kernel, labels, row_count):
    tap_count = kernel.shape[0]
    half_width = tap_count // 2
    centre = labels[half_width : half_width + row_count]
    result = jnp.zeros((row_count, kernel.shape[1]), jnp.float32)
    for tap_index in range(tap_count):
        tap_row = 2 * half_width - tap_index
        same_utt = (labels[tap_row : tap_row + row_count] == centre).astype(jnp.float32)
        result = (
            result + kernel[tap_index] * window[tap_row : tap_row + row_count] * same_utt[:, None]
        )
    return result


def finish(d_glu, values, gates, hidden, normed, scale_inv, backward_product):
    d_mixed = jnp.concatenate(
        [d_glu * gates, d_glu * values * gates * (1.0 - gates)], axis=1
    ).astype(jnp.bfloat16)
    d_hidden = backward_product(d_mixed)
    d_rows = norm_backward(d_hidden, normed, scale_inv).astype(jnp.bfloat16)
    partial_sum = lax.dot_general(
        hidden, d_mixed, (((0,), (0,)), ((), ())), preferred_element_type=jnp.float32
    )
    return (d_rows, partial_sum)


def on_device(frames, lengths, offsets, w_in, kernel, cotangent):
    rows_in = frames[0]
    per_device = rows_in.shape[0]
    model_width = rows_in.shape[1]
    capacity = 2 * per_device
    seq_count = lax.axis_size("seq")
    group_count = lax.axis_size("fsdp")
    device = lax.axis_index("seq")
    frame_total = seq_count * per_device
    half_width = kernel.shape[0] // 2
    bounds_row = offsets[0]
    start_row = bounds_row[device]
    owned_load = bounds_row[device + 1] - start_row
    base_row = (device - 1) * per_device
    utt_bounds = jnp.cumsum(lengths[0])[:-1]
    slot_index = jnp.arange(capacity, dtype=jnp.int32)
    owned = (slot_index < owned_load)[:, None]
    bf_zero = jnp.zeros((), jnp.bfloat16)
    cot_rows = jnp.where(owned, cotangent[0], bf_zero)

    def backward_product(d_mixed):
        return lax.dot_general(
            d_mixed,
            lax.all_gather(w_in, "fsdp", axis=0, tiled=True),
            (((1,), (1,)), ((), ())),
            preferred_element_type=jnp.float32,
        )

    from_prev = passed_along(rows_in, "seq", 1)
    from_next = passed_along(rows_in, "seq", -1)
    gathered = jnp.concatenate([from_prev, rows_in, from_next, jnp.zeros_like(rows_in)], axis=0)
    window_rows = capacity + 2 * half_width
    rows_window = lax.dynamic_slice_in_dim(
        gathered, start_row - half_width - base_row, window_rows, 0
    )
    positions = start_row - half_width + jnp.arange(window_rows, dtype=jnp.int32)
    labels = jnp.sum((positions[:, None] >= utt_bounds[None, :]).astype(jnp.int32), axis=1)
    inside = (positions >= 0) & (positions < frame_total)
    labels = jnp.where(inside, labels, -1)
    normed, scale_inv = normalize_rows(rows_window)
    hidden = normed.astype(jnp.bfloat16)
    projected = jnp.dot(
        hidden, lax.all_gather(w_in, "fsdp", axis=0, tiled=True), preferred_element_type=jnp.float32
    )
    values = projected[:, :model_width]
    gates = jax.nn.sigmoid(projected[:, model_width:])
    glu_out = (values * gates).astype(jnp.bfloat16)
    conv = depthwise(glu_out, kernel, labels, capacity)
    conv_normed, conv_inv = normalize_rows(conv)
    gate_out = jax.nn.sigmoid(conv_normed)
    output = conv_normed * gate_out
    owner_output = jnp.where(owned, output.astype(jnp.bfloat16), bf_zero)
    upstream = cot_rows.astype(jnp.float32)
    d_normed = upstream * (gate_out + output * (1.0 - gate_out))
    d_conv = jnp.where(owned, norm_backward(d_normed, conv_normed, conv_inv), 0.0)
    tail_rows = lax.dynamic_slice_in_dim(d_conv, owned_load - half_width, half_width, 0)
    head_rows = d_conv[:half_width]
    left_part = passed_along(tail_rows.astype(jnp.bfloat16), "seq", 1).astype(tail_rows.dtype)
    right_part = passed_along(head_rows.astype(jnp.bfloat16), "seq", -1).astype(head_rows.dtype)
    edge_zeros = jnp.zeros((half_width, model_width), jnp.float32)
    d_window = jnp.concatenate([left_part, d_conv, edge_zeros], axis=0)
    right_placed = lax.dynamic_update_slice_in_dim(
        jnp.zeros((window_rows, model_width), jnp.float32), right_part, half_width + owned_load, 0
    )
    d_window = d_window + right_placed
    d_glu = jnp.where(owned, depthwise_back(d_window, kernel, labels, capacity), 0.0)
    inner_end = half_width + capacity
    d_rows, partial_sum = finish(
        d_glu,
        values[half_width:inner_end],
        gates[half_width:inner_end],
        hidden[half_width:inner_end],
        normed[half_width:inner_end],
        scale_inv[half_width:inner_end],
        backward_product,
    )
    placed = lax.dynamic_update_slice_in_dim(
        jnp.zeros((4 * per_device, model_width), jnp.bfloat16), d_rows, start_row - base_row, 0
    )
    back_prev = passed_along(placed[:per_device], "seq", -1)
    back_next = passed_along(placed[2 * per_device : 3 * per_device], "seq", 1)
    frame_grad = (
        placed[per_device : 2 * per_device].astype(jnp.float32)
        + back_prev.astype(jnp.float32)
        + back_next.astype(jnp.float32)
    ).astype(jnp.bfloat16)
    rounded = lax.optimization_barrier(partial_sum.astype(jnp.bfloat16)).astype(jnp.float32)
    seq_summed = lax.psum_scatter(
        rounded.astype(jnp.bfloat16), "seq", scatter_dimension=0, tiled=True
    )
    summed = lax.psum_scatter(seq_summed, "fsdp", scatter_dimension=0, tiled=True).astype(
        jnp.float32
    )
    w_grad = summed * (1.0 / math.sqrt(group_count * frame_total))
    return (owner_output[None], frame_grad[None], w_grad)


def solution(mesh):
    return jax.shard_map(
        on_device,
        mesh=mesh,
        in_specs=(
            P("fsdp", "seq", None),
            P("fsdp", None),
            P("fsdp", None),
            P("fsdp", None),
            P(),
            P("fsdp", "seq", None),
        ),
        out_specs=(P("fsdp", "seq", None), P("fsdp", "seq", None), P(("seq", "fsdp"), None)),
        check_vma=False,
    )
```

profile of v0, /device:TPU:8, one launch (start us, length us, event | category | flops | bytes accessed | tf_op | source)
XLA Modules:
  0.0 391.4 jit_solution(15712493318630391508)
XLA Ops:
  8.0 3.8 collective-permute-start
  11.8 1.3 collective-permute-start.1
  13.1 1.4 constant_dynamic-slice_fusion.1
  17.6 1.6 slice_reduce_fusion.29
  20.8 1.8 slice_reduce_fusion.30
  23.4 1.3 collective-permute-done.1
  26.0 1.5 fusion.1
  27.6 41.1 %all-gather.2.cloned.1.call-done = bf16[1536,3072]{1,0:T(8,128)(2,1)} async-done(((bf16[192,3072]{1,0:T(8,128)(2,1)}), bf16[1536,3072]{1,0:T(8,128)(2,1)}) %all-gather.2.cloned.1.call-update) | async-done | bytes 9437200 | tf_op jit(solution)/shard_map/all_gather | solution.py:114
  68.7 5.4 %fusion.90 = f32[286,3072]{1,0:T(8,128)S(1)} fusion(bf16[286,1536]{1,0:T(8,128)(2,1)S(1)} %get-tuple-element.52, bf16[1536,3072]{1,0:T(8,128)(2,1)} %all-gather.2.cloned.1.call-done), kind=kOutput, calls=%fused_computation.223 | convolution fusion | flops 2699034624 | bytes 13830144 | tf_op jit(solution)/shard_map/dot_general | solution.py:113
  74.2 2.1 fusion.6
  76.9 13.3 %fusion.86 = (f32[256]{0:T(256)S(1)}, f32[256,1536]{1,0:T(8,128)S(1)}) fusion(f32[256]{0:T(256)S(1)} %get-tuple-element.82, bf16[286,1536]{1,0:T(8,128)(2,1)S(1)} %get-tuple-element.46, f32[1536]{0:T(1024)S(1)} %get-tuple-element.36, f32[256]{0:T(256)S(1)} %get-tuple-element.54, f32[1536]{0:T(1024)S(1)} %get-tuple-element.37, f32[256]{0:T(256)S(1)} %get-tuple-element.55, ...), kind=kLoop, calls=%fused_computation.220 | loop fusion | flops 48365312 | bytes 26174464 | tf_op jit(solution)/shard_map/reduce_sum | solution.py:18
  91.3 1.7 fusion.84
  93.0 1.1 multiply_select_fusion
  94.2 1.1 copy-done.2
  95.3 3.5 collective-permute-start.2
  99.5 1.5 collective-permute-start.3
  101.0 1.6 maximum_maximum_fusion
  102.6 2.9 collective-permute-done.3
  106.2 10.6 %multiply_convert_fusion.1 = (bf16[256,1536]{1,0:T(8,128)(2,1)S(1)}, f32[256,1536]{1,0:T(8,128)S(1)}) fusion(f32[286,1536]{1,0:T(8,128)} %get-tuple-element.45, f32[256]{0:T(256)} %copy-done.37, f32[286,1536]{1,0:T(8,128)S(1)} %add.319, f32[1536]{0:T(1024)} %copy-done.26, f32[256]{0:T(256)} %copy-done.46, f32[1536]{0:T(1024)} %copy-done.27, ...), kind=kLoop, calls=%fused_computation.115 | loop fusion | flops 36962304 | bytes 52912384 | tf_op jit(solution)/shard_map/convert
  116.9 2.3 fusion.10
  120.0 5.2 %convolution_convert_fusion = bf16[1536,3072]{1,0:T(8,128)(2,1)} fusion(bf16[256,1536]{1,0:T(8,128)(2,1)S(1)} %fusion.10, bf16[256,1536]{1,0:T(8,128)(2,1)S(1)} %get-tuple-element.38, bf16[286,1536]{1,0:T(8,128)(2,1)S(1)} %copy-done.6), kind=kOutput, calls=%fused_computation | convolution fusion | flops 2423783424 | bytes 11796480 | tf_op jit(solution)/shard_map/dot_general | solution.py:66
  127.5 2.1 select_bitcast_fusion
  129.5 5.9 %fusion.83 = (f32[256]{0:T(256)S(1)}, f32[256]{0:T(256)S(1)}, f32[256,1536]{1,0:T(8,128)S(1)}) fusion(f32[286,1536]{1,0:T(8,128)S(1)} %copy-done.3, bf16[1536,3072]{1,0:T(8,128)(2,1)} %all-gather.2.cloned.1.call-done, bf16[256,1536]{1,0:T(8,128)(2,1)} %copy-done.8, bf16[256,1536]{1,0:T(8,128)(2,1)} %copy-done.9), kind=kOutput, calls=%fused_computation.218 | convolution fusion | flops 2420243968 | bytes 14157824 | tf_op jit(solution)/shard_map/dot_general | solution.py:93
  135.5 1.3 multiply_convert_fusion
  137.9 4.0 %dynamic_update_slice.7 = bf16[512,1536]{1,0:T(8,128)(2,1)S(1)} dynamic-update-slice(bf16[512,1536]{1,0:T(8,128)(2,1)S(1)} %broadcast_in_dim.45, bf16[256,1536]{1,0:T(8,128)(2,1)S(1)} %copy-done.4, s32[]{:T(128)S(6)} %select_n.46, s32[]{:T(128)} %constant.22.clone.1) | dynamic-update-slice | bytes 1572868 | tf_op jit(solution)/shard_map/dynamic_update_slice | solution.py:148
  141.9 1.3 collective-permute-start.4
  143.2 4.6 %collective-permute-start.5 = (bf16[128,1536]{1,0:T(8,128)(2,1)S(1)}, bf16[128,1536]{1,0:T(8,128)(2,1)S(1)}, u32[]{:S(2)}, u32[]{:S(2)}) collective-permute-start(bf16[128,1536]{1,0:T(8,128)(2,1)S(1)} %get-tuple-element.48), channel_id=1, source_target_pairs={{0,8},{8,16},{16,24},{24,32},{32,40},{40,48},{48,56},{56,64},{64,7... | collective-permute-start | bytes 1179656 | tf_op jit(solution)/shard_map/ppermute | solution.py:13
  147.8 212.4 %reduce-scatter.4.cloned.1.call-done = bf16[48,3072]{1,0:T(8,128)(2,1)} async-done(((bf16[1536,3072]{1,0:T(8,128)(2,1)}), bf16[48,3072]{1,0:T(8,128)(2,1)}) %reduce-scatter.4.cloned.1.call-update) | async-done | bytes 294928 | tf_op jit(solution)/shard_map/reduce_scatter | solution.py:159
  360.2 14.8 %fusion = bf16[8,3072]{1,0:T(8,128)(2,1)S(1)} fusion(bf16[48,3072]{1,0:T(8,128)(2,1)} %reduce-scatter.4.cloned.1.call-done), kind=kCustom, calls=%all-reduce-scatter | all-reduce-scatter fusion | flops 196609 | bytes 345088
  375.0 1.9 collective-permute-start.6
  376.9 2.1 collective-permute-start.7
  379.9 3.6 collective-permute-done.7
  (152 shorter events, 12.9 us)
Async XLA Ops:
  7.2 61.5 %all-gather.2.cloned.1.call-start = ((), (), s32[]{:S(2)}) async-start(), calls=%async_computation.1 | async-start | bytes 10616832 | tf_op jit(solution)/shard_map/all_gather | solution.py:114
  7.9 352.3 %reduce-scatter.4.cloned.1.call-start = ((), (), s32[]{:S(2)}) async-start(), calls=%async_computation.2 | async-start | bytes 9732096 | tf_op jit(solution)/shard_map/reduce_scatter | solution.py:159
  8.0 15.4 %collective-permute-start = (bf16[128,1536]{1,0:T(8,128)(2,1)}, bf16[128,1536]{1,0:T(8,128)(2,1)S(1)}, u32[]{:S(2)}, u32[]{:S(2)}) collective-permute-start(bf16[128,1536]{1,0:T(8,128)(2,1)} %bitcast.21), channel_id=1, source_target_pairs={{0,8},{8,16},{16,24},{24,32},{32,40},{40,48},{48,56},{56,64},{64,7... | collective-permute-start | bytes 1179656 | tf_op jit(solution)/shard_map/ppermute | solution.py:13
  11.8 12.8 %collective-permute-start.1 = (bf16[128,1536]{1,0:T(8,128)(2,1)}, bf16[128,1536]{1,0:T(8,128)(2,1)S(1)}, u32[]{:S(2)}, u32[]{:S(2)}) collective-permute-start(bf16[128,1536]{1,0:T(8,128)(2,1)} %bitcast.22), channel_id=1, source_target_pairs={{8,0},{16,8},{24,16},{32,24},{40,32},{48,40},{56,48},{64,56},{72,6... | collective-permute-start | bytes 1179656 | tf_op jit(solution)/shard_map/ppermute | solution.py:13
  19.2 57.3 %copy-start.16 = (f32[1536]{0:T(1024)}, f32[1536]{0:T(1024)S(1)}, u32[]{:S(2)}) copy-start(f32[1536]{0:T(1024)S(1)} %get-tuple-element.26) | copy-start | bytes 18436
  19.2 57.3 %copy-start.17 = (f32[1536]{0:T(1024)}, f32[1536]{0:T(1024)S(1)}, u32[]{:S(2)}) copy-start(f32[1536]{0:T(1024)S(1)} %get-tuple-element.27) | copy-start | bytes 18436
  19.2 57.3 %copy-start.18 = (f32[1536]{0:T(1024)}, f32[1536]{0:T(1024)S(1)}, u32[]{:S(2)}) copy-start(f32[1536]{0:T(1024)S(1)} %get-tuple-element.28) | copy-start | bytes 18436
  19.2 57.3 %copy-start.19 = (f32[1536]{0:T(1024)}, f32[1536]{0:T(1024)S(1)}, u32[]{:S(2)}) copy-start(f32[1536]{0:T(1024)S(1)} %get-tuple-element.29) | copy-start | bytes 18436
  19.3 57.3 %copy-start.20 = (f32[1536]{0:T(1024)}, f32[1536]{0:T(1024)S(1)}, u32[]{:S(2)}) copy-start(f32[1536]{0:T(1024)S(1)} %get-tuple-element.30) | copy-start | bytes 18436
  19.3 57.3 %copy-start.21 = (f32[1536]{0:T(1024)}, f32[1536]{0:T(1024)S(1)}, u32[]{:S(2)}) copy-start(f32[1536]{0:T(1024)S(1)} %get-tuple-element.31) | copy-start | bytes 18436
  19.3 57.3 %copy-start.22 = (f32[1536]{0:T(1024)}, f32[1536]{0:T(1024)S(1)}, u32[]{:S(2)}) copy-start(f32[1536]{0:T(1024)S(1)} %get-tuple-element.32) | copy-start | bytes 18436
  19.3 57.3 %copy-start.23 = (f32[1536]{0:T(1024)}, f32[1536]{0:T(1024)S(1)}, u32[]{:S(2)}) copy-start(f32[1536]{0:T(1024)S(1)} %get-tuple-element.33) | copy-start | bytes 18436
  19.3 57.3 %copy-start.24 = (f32[1536]{0:T(1024)}, f32[1536]{0:T(1024)S(1)}, u32[]{:S(2)}) copy-start(f32[1536]{0:T(1024)S(1)} %get-tuple-element.34) | copy-start | bytes 18436
  19.3 57.3 %copy-start.25 = (f32[1536]{0:T(1024)}, f32[1536]{0:T(1024)S(1)}, u32[]{:S(2)}) copy-start(f32[1536]{0:T(1024)S(1)} %get-tuple-element.35) | copy-start | bytes 18436
  19.3 57.3 %copy-start.26 = (f32[1536]{0:T(1024)}, f32[1536]{0:T(1024)S(1)}, u32[]{:S(2)}) copy-start(f32[1536]{0:T(1024)S(1)} %get-tuple-element.36) | copy-start | bytes 18436
  19.3 57.3 %copy-start.27 = (f32[1536]{0:T(1024)}, f32[1536]{0:T(1024)S(1)}, u32[]{:S(2)}) copy-start(f32[1536]{0:T(1024)S(1)} %get-tuple-element.37) | copy-start | bytes 18436
  19.4 57.2 %copy-start.34 = (f32[256]{0:T(256)}, f32[256]{0:T(256)S(1)}, u32[]{:S(2)}) copy-start(f32[256]{0:T(256)S(1)} %get-tuple-element.80) | copy-start | bytes 3076
  19.4 57.2 %copy-start.35 = (f32[256]{0:T(256)}, f32[256]{0:T(256)S(1)}, u32[]{:S(2)}) copy-start(f32[256]{0:T(256)S(1)} %get-tuple-element.81) | copy-start | bytes 3076
  19.4 57.2 %copy-start.36 = (f32[256]{0:T(256)}, f32[256]{0:T(256)S(1)}, u32[]{:S(2)}) copy-start(f32[256]{0:T(256)S(1)} %get-tuple-element.82) | copy-start | bytes 3076
  19.5 57.2 %copy-start.37 = (f32[256]{0:T(256)}, f32[256]{0:T(256)S(1)}, u32[]{:S(2)}) copy-start(f32[256]{0:T(256)S(1)} %get-tuple-element.53) | copy-start | bytes 3076
  19.5 57.2 %copy-start.38 = (f32[256]{0:T(256)}, f32[256]{0:T(256)S(1)}, u32[]{:S(2)}) copy-start(f32[256]{0:T(256)S(1)} %get-tuple-element.54) | copy-start | bytes 3076
  19.5 57.2 %copy-start.39 = (f32[256]{0:T(256)}, f32[256]{0:T(256)S(1)}, u32[]{:S(2)}) copy-start(f32[256]{0:T(256)S(1)} %get-tuple-element.55) | copy-start | bytes 3076
  19.5 57.2 %copy-start.40 = (f32[256]{0:T(256)}, f32[256]{0:T(256)S(1)}, u32[]{:S(2)}) copy-start(f32[256]{0:T(256)S(1)} %get-tuple-element.56) | copy-start | bytes 3076
  19.6 57.2 %copy-start.41 = (f32[256]{0:T(256)}, f32[256]{0:T(256)S(1)}, u32[]{:S(2)}) copy-start(f32[256]{0:T(256)S(1)} %get-tuple-element.57) | copy-start | bytes 3076
  19.6 57.2 %copy-start.42 = (f32[256]{0:T(256)}, f32[256]{0:T(256)S(1)}, u32[]{:S(2)}) copy-start(f32[256]{0:T(256)S(1)} %get-tuple-element.58) | copy-start | bytes 3076
  19.6 57.2 %copy-start.43 = (f32[256]{0:T(256)}, f32[256]{0:T(256)S(1)}, u32[]{:S(2)}) copy-start(f32[256]{0:T(256)S(1)} %get-tuple-element.59) | copy-start | bytes 3076
  95.3 5.6 %collective-permute-start.2 = (bf16[15,1536]{1,0:T(8,128)(2,1)S(1)}, bf16[15,1536]{1,0:T(8,128)(2,1)S(1)}, u32[]{:S(2)}, u32[]{:S(2)}) collective-permute-start(bf16[15,1536]{1,0:T(8,128)(2,1)S(1)} %get-tuple-element.50), channel_id=1, source_target_pairs={{0,8},{8,16},{16,24},{24,32},{32,40},{40,48},{48,56},{56,64},{64,7... | collective-permute-start | bytes 138248 | tf_op jit(solution)/shard_map/ppermute | solution.py:13
  99.5 6.0 %collective-permute-start.3 = (bf16[15,1536]{1,0:T(8,128)(2,1)S(1)}, bf16[15,1536]{1,0:T(8,128)(2,1)S(1)}, u32[]{:S(2)}, u32[]{:S(2)}) collective-permute-start(bf16[15,1536]{1,0:T(8,128)(2,1)S(1)} %get-tuple-element.49), channel_id=1, source_target_pairs={{8,0},{16,8},{24,16},{32,24},{40,32},{48,40},{56,48},{64,56},{72,6... | collective-permute-start | bytes 138248 | tf_op jit(solution)/shard_map/ppermute | solution.py:13
  141.9 237.1 %collective-permute-start.4 = (bf16[128,1536]{1,0:T(8,128)(2,1)S(1)}, bf16[128,1536]{1,0:T(8,128)(2,1)S(1)}, u32[]{:S(2)}, u32[]{:S(2)}) collective-permute-start(bf16[128,1536]{1,0:T(8,128)(2,1)S(1)} %get-tuple-element.47), channel_id=1, source_target_pairs={{8,0},{16,8},{24,16},{32,24},{40,32},{48,40},{56,48},{64,56},{72,6... | collective-permute-start | bytes 1179656 | tf_op jit(solution)/shard_map/ppermute | solution.py:13
  143.2 235.8 %collective-permute-start.5 = (bf16[128,1536]{1,0:T(8,128)(2,1)S(1)}, bf16[128,1536]{1,0:T(8,128)(2,1)S(1)}, u32[]{:S(2)}, u32[]{:S(2)}) collective-permute-start(bf16[128,1536]{1,0:T(8,128)(2,1)S(1)} %get-tuple-element.48), channel_id=1, source_target_pairs={{0,8},{8,16},{16,24},{24,32},{32,40},{40,48},{48,56},{56,64},{64,7... | collective-permute-start | bytes 1179656 | tf_op jit(solution)/shard_map/ppermute | solution.py:13
  375.0 8.5 %collective-permute-start.6 = (bf16[8,3072]{1,0:T(8,128)(2,1)S(1)}, bf16[8,3072]{1,0:T(8,128)(2,1)S(1)}, u32[]{:S(2)}, u32[]{:S(2)}) collective-permute-start(bf16[8,3072]{1,0:T(8,128)(2,1)S(1)} %fusion), channel_id=1, source_target_pairs={{0,1},{1,2},{2,3},{3,4},{4,5},{5,6},{6,7},{8,9},{9,10},{10,11},{11... | collective-permute-start | bytes 147464
  376.9 6.6 %collective-permute-start.7 = (bf16[6,3072]{1,0:T(8,128)(2,1)S(1)}, bf16[6,3072]{1,0:T(8,128)(2,1)S(1)}, u32[]{:S(2)}, u32[]{:S(2)}) collective-permute-start(bf16[6,3072]{1,0:T(8,128)(2,1)S(1)} %slice.684), channel_id=1, source_target_pairs={{0,2},{1,3},{2,4},{3,5},{4,6},{5,7},{8,10},{9,11},{10,12},{11,13},... | collective-permute-start | bytes 110600
  (32 other events, 885.8 us)
Sparse Core Ops, SparseCore 0:
  9.8 58.8 all-gather.1
  125.4 234.7 reduce-scatter.3
where the time goes:
time: 392 us; the launch traced here: 391 us
  waiting for transfers between devices  262 us (67%)
  other arithmetic  43.6 us (11%)
  starting transfers between devices  20 us (5%)
  between operations  18.5 us (5%)
  matrix products  16.6 us (4%)
  local copies, waits for them, and re-layouts  15.9 us (4%)
  blocking collectives  14.8 us (4%)
    reduce_scatter x1, waiting for transfers between devices, on_device(): lax.psum_scatter(rounded.astype(jnp.bfloat16), 'seq', scatter_dimension=0...  212 us
    all_gather x1, waiting for transfers between devices, on_device(): lax.all_gather(w_in, 'fsdp', axis=0, tiled=True)  41.1 us
    ppermute x6, starting transfers between devices, passed_along(): lax.ppermute(value, axis, [(source, source + steps) for source in range(i...  15.9 us
    unnamed x1, blocking collectives  14.8 us
    reduce_sum x2, other arithmetic, normalize_rows(): center = jnp.mean(values, axis=-1, keepdims=True)  14.2 us
    another operation x3, other arithmetic  13.7 us
  transfers between devices with their start and end apart: 10, of which 5 were waited for; matrix products, arithmetic and copies ran while one was open for 11% of the time, Pallas kernels for 0%

commit v1 on v0

--- a/solution.py
+++ b/solution.py
@@ -111,7 +111,11 @@
     normed, scale_inv = normalize_rows(rows_window)
     hidden = normed.astype(jnp.bfloat16)
     projected = jnp.dot(
-        hidden, lax.all_gather(w_in, "fsdp", axis=0, tiled=True), preferred_element_type=jnp.float32
+        hidden,
+        jnp.concatenate(
+            lax.all_to_all(jnp.stack([w_in] * lax.axis_size("fsdp")), "fsdp", 0, 0), axis=0
+        ),
+        preferred_element_type=jnp.float32,
     )
     values = projected[:, :model_width]
     gates = jax.nn.sigmoid(projected[:, model_width:])

time: 392 us -> 487 us (1.24)
  waiting for transfers between devices: 262 us -> 350 us
    all_to_all x0 -> x1, waiting for transfers between devices: none -> 124 us  [on_device(): lax.all_to_all(jnp.stack([w_in] * lax.axis_size('fsdp')), 'fsdp', 0, 0)]
    all_gather x1, waiting for transfers between devices: 41.1 us -> 0.01 us  [backward_product(): lax.all_gather(w_in, 'fsdp', axis=0, tiled=True)]
    all_to_all x0 -> x1, starting transfers between devices: none -> 7.24 us  [on_device(): lax.all_to_all(jnp.stack([w_in] * lax.axis_size('fsdp')), 'fsdp', 0, 0)]
    another operation x0 -> x1, local copies, waits for them, and re-layouts: none -> 6.19 us  [on_device(): jnp.stack([w_in] * lax.axis_size('fsdp'))]
  transfers between devices with their start and end apart: 10 -> 11, of which waited for: 5 -> 6; matrix products, arithmetic and copies ran while one was open for 11% -> 17% of each run, Pallas kernels for 0% -> 0%
where the time goes in v1:
time: 487 us
  waiting for transfers between devices  350 us (72%)
  other arithmetic  43.1 us (9%)
  starting transfers between devices  24.2 us (5%)
  between operations  19.8 us (4%)
  local copies, waits for them, and re-layouts  18.4 us (4%)
  matrix products  16.6 us (3%)
  blocking collectives  14.7 us (3%)
    reduce_scatter x1, waiting for transfers between devices, on_device(): lax.psum_scatter(rounded.astype(jnp.bfloat16), 'seq', scatter_dimension=0...  213 us
    all_to_all x1, waiting for transfers between devices, on_device(): lax.all_to_all(jnp.stack([w_in] * lax.axis_size('fsdp')), 'fsdp', 0, 0)  124 us
    unnamed x1, blocking collectives  14.7 us
    reduce_sum x2, other arithmetic, normalize_rows(): center = jnp.mean(values, axis=-1, keepdims=True)  14.2 us
    another operation x3, other arithmetic  13 us
    ppermute x6, starting transfers between devices, passed_along(): lax.ppermute(value, axis, [(source, source + steps) for source in range(i...  12.8 us
  transfers between devices with their start and end apart: 11, of which 6 were waited for; matrix products, arithmetic and copies ran while one was open for 17% of the time, Pallas kernels for 0%

profile of v1, /device:TPU:8, one launch (start us, length us, event | category | flops | bytes accessed | tf_op | source)
XLA Modules:
  0.0 486.7 jit_solution(5899099318138466437)
XLA Ops:
  8.0 6.2 %stack.2 = bf16[8,192,3072]{2,1,0:T(8,128)(2,1)} broadcast(bf16[192,3072]{1,0:T(8,128)(2,1)} %param.9), dimensions={1,2} | broadcast | bytes 10616832 | tf_op jit(solution)/shard_map/stack | solution.py:116
  14.2 7.2 %all-to-all-start = ((bf16[8,192,3072]{2,1,0:T(8,128)(2,1)}), bf16[8,192,3072]{2,1,0:T(8,128)(2,1)}, u32[]{:S(2)}, u32[]{:S(2)}) async-start(bf16[8,192,3072]{2,1,0:T(8,128)(2,1)} %stack.2), calls=%async_computation | async-start | bytes 18874368 | tf_op jit(solution)/shard_map/all_to_all | solution.py:116
  22.2 2.1 collective-permute-start
  24.3 1.3 collective-permute-start.1
  31.5 1.5 collective-permute-done
  33.0 4.3 collective-permute-done.1
  38.6 1.6 fusion.1
  40.2 123.7 %all-to-all-done = bf16[8,192,3072]{2,1,0:T(8,128)(2,1)} async-done(((bf16[8,192,3072]{2,1,0:T(8,128)(2,1)}), bf16[8,192,3072]{2,1,0:T(8,128)(2,1)}, u32[]{:S(2)}, u32[]{:S(2)}) %all-to-all-start) | async-done | bytes 9437216 | tf_op jit(solution)/shard_map/all_to_all | solution.py:116
  163.9 5.4 %fusion.90 = f32[286,3072]{1,0:T(8,128)S(1)} fusion(bf16[286,1536]{1,0:T(8,128)(2,1)S(1)} %get-tuple-element.52, bf16[1536,3072]{1,0:T(8,128)(2,1)} %bitcast.3), kind=kOutput, calls=%fused_computation.223 | convolution fusion | flops 2699034624 | bytes 13830144 | tf_op jit(solution)/shard_map/dot_general | solution.py:113
  169.3 2.1 fusion.6
  172.1 13.3 %fusion.86 = (f32[256]{0:T(256)S(1)}, f32[256,1536]{1,0:T(8,128)S(1)}) fusion(f32[256]{0:T(256)S(1)} %get-tuple-element.82, bf16[286,1536]{1,0:T(8,128)(2,1)S(1)} %get-tuple-element.46, f32[1536]{0:T(1024)S(1)} %get-tuple-element.36, f32[256]{0:T(256)S(1)} %get-tuple-element.54, f32[1536]{0:T(1024)S(1)} %get-tuple-element.37, f32[256]{0:T(256)S(1)} %get-tuple-element.55, ...), kind=kLoop, calls=%fused_computation.220 | loop fusion | flops 48365312 | bytes 26174464 | tf_op jit(solution)/shard_map/reduce_sum | solution.py:18
  186.5 1.7 fusion.84
  188.2 1.1 multiply_select_fusion
  189.4 1.1 copy-done.2
  190.5 2.1 collective-permute-start.2
  193.3 1.5 collective-permute-start.3
  194.8 1.6 maximum_maximum_fusion
  196.4 2.9 collective-permute-done.3
  200.1 10.6 %multiply_convert_fusion.1 = (bf16[256,1536]{1,0:T(8,128)(2,1)S(1)}, f32[256,1536]{1,0:T(8,128)S(1)}) fusion(f32[286,1536]{1,0:T(8,128)} %get-tuple-element.45, f32[256]{0:T(256)} %copy-done.38, f32[286,1536]{1,0:T(8,128)S(1)} %add.319, f32[1536]{0:T(1024)} %copy-done.27, f32[256]{0:T(256)} %copy-done.47, f32[1536]{0:T(1024)} %copy-done.28, ...), kind=kLoop, calls=%fused_computation.115 | loop fusion | flops 36962304 | bytes 52912384 | tf_op jit(solution)/shard_map/convert
  210.7 2.3 fusion.10
  213.9 5.2 %convolution_convert_fusion = bf16[1536,3072]{1,0:T(8,128)(2,1)} fusion(bf16[256,1536]{1,0:T(8,128)(2,1)S(1)} %fusion.10, bf16[256,1536]{1,0:T(8,128)(2,1)S(1)} %get-tuple-element.38, bf16[286,1536]{1,0:T(8,128)(2,1)S(1)} %copy-done.6), kind=kOutput, calls=%fused_computation | convolution fusion | flops 2423783424 | bytes 11796480 | tf_op jit(solution)/shard_map/dot_general | solution.py:66
  221.2 2.1 select_bitcast_fusion
  223.3 5.9 %fusion.83 = (f32[256]{0:T(256)S(1)}, f32[256]{0:T(256)S(1)}, f32[256,1536]{1,0:T(8,128)S(1)}) fusion(f32[286,1536]{1,0:T(8,128)S(1)} %copy-done.3, bf16[1536,3072]{1,0:T(8,128)(2,1)} %all-gather.2.cloned.1.call-done, bf16[256,1536]{1,0:T(8,128)(2,1)} %copy-done.8, bf16[256,1536]{1,0:T(8,128)(2,1)} %copy-done.9), kind=kOutput, calls=%fused_computation.218 | convolution fusion | flops 2420243968 | bytes 14157824 | tf_op jit(solution)/shard_map/dot_general | solution.py:93
  229.2 1.3 multiply_convert_fusion
  231.7 4.0 dynamic_update_slice.7
  235.7 1.3 collective-permute-start.4
  237.0 4.6 collective-permute-start.5
  241.6 213.4 %reduce-scatter.4.cloned.1.call-done = bf16[48,3072]{1,0:T(8,128)(2,1)} async-done(((bf16[1536,3072]{1,0:T(8,128)(2,1)}), bf16[48,3072]{1,0:T(8,128)(2,1)}) %reduce-scatter.4.cloned.1.call-update) | async-done | bytes 294928 | tf_op jit(solution)/shard_map/reduce_scatter | solution.py:163
  455.0 14.7 %fusion = bf16[8,3072]{1,0:T(8,128)(2,1)S(1)} fusion(bf16[48,3072]{1,0:T(8,128)(2,1)} %reduce-scatter.4.cloned.1.call-done), kind=kCustom, calls=%all-reduce-scatter | all-reduce-scatter fusion | flops 196609 | bytes 345088
  469.7 1.9 collective-permute-start.6
  471.6 2.2 collective-permute-start.7
  474.7 3.5 collective-permute-done.7
  (161 shorter events, 13.5 us)
Async XLA Ops:
  14.2 149.7 %all-to-all-start = ((bf16[8,192,3072]{2,1,0:T(8,128)(2,1)}), bf16[8,192,3072]{2,1,0:T(8,128)(2,1)}, u32[]{:S(2)}, u32[]{:S(2)}) async-start(bf16[8,192,3072]{2,1,0:T(8,128)(2,1)} %stack.2), calls=%async_computation | async-start | bytes 18874368 | tf_op jit(solution)/shard_map/all_to_all | solution.py:116
  21.4 201.9 %all-gather.2.cloned.1.call-start = ((), (), s32[]{:S(2)}) async-start(), calls=%async_computation.2 | async-start | bytes 10616832 | tf_op jit(solution)/shard_map/all_gather | solution.py:95
  22.2 432.8 %reduce-scatter.4.cloned.1.call-start = ((), (), s32[]{:S(2)}) async-start(), calls=%async_computation.3 | async-start | bytes 9732096 | tf_op jit(solution)/shard_map/reduce_scatter | solution.py:163
  22.2 10.8 %collective-permute-start = (bf16[128,1536]{1,0:T(8,128)(2,1)S(1)}, bf16[128,1536]{1,0:T(8,128)(2,1)S(1)}, u32[]{:S(2)}, u32[]{:S(2)}) collective-permute-start(bf16[128,1536]{1,0:T(8,128)(2,1)S(1)} %bitcast.22), channel_id=1, source_target_pairs={{0,8},{8,16},{16,24},{24,32},{32,40},{40,48},{48,56},{56,64},{64,7... | collective-permute-start | bytes 1179656 | tf_op jit(solution)/shard_map/ppermute | solution.py:13
  24.3 12.9 %collective-permute-start.1 = (bf16[128,1536]{1,0:T(8,128)(2,1)S(1)}, bf16[128,1536]{1,0:T(8,128)(2,1)S(1)}, u32[]{:S(2)}, u32[]{:S(2)}) collective-permute-start(bf16[128,1536]{1,0:T(8,128)(2,1)S(1)} %bitcast.23), channel_id=1, source_target_pairs={{8,0},{16,8},{24,16},{32,24},{40,32},{48,40},{56,48},{64,56},{72,6... | collective-permute-start | bytes 1179656 | tf_op jit(solution)/shard_map/ppermute | solution.py:13
  28.8 142.9 %copy-start.17 = (f32[1536]{0:T(1024)}, f32[1536]{0:T(1024)S(1)}, u32[]{:S(2)}) copy-start(f32[1536]{0:T(1024)S(1)} %get-tuple-element.26) | copy-start | bytes 18436
  28.8 142.9 %copy-start.18 = (f32[1536]{0:T(1024)}, f32[1536]{0:T(1024)S(1)}, u32[]{:S(2)}) copy-start(f32[1536]{0:T(1024)S(1)} %get-tuple-element.27) | copy-start | bytes 18436
  28.8 142.9 %copy-start.19 = (f32[1536]{0:T(1024)}, f32[1536]{0:T(1024)S(1)}, u32[]{:S(2)}) copy-start(f32[1536]{0:T(1024)S(1)} %get-tuple-element.28) | copy-start | bytes 18436
  28.8 142.9 %copy-start.20 = (f32[1536]{0:T(1024)}, f32[1536]{0:T(1024)S(1)}, u32[]{:S(2)}) copy-start(f32[1536]{0:T(1024)S(1)} %get-tuple-element.29) | copy-start | bytes 18436
  28.8 142.9 %copy-start.21 = (f32[1536]{0:T(1024)}, f32[1536]{0:T(1024)S(1)}, u32[]{:S(2)}) copy-start(f32[1536]{0:T(1024)S(1)} %get-tuple-element.30) | copy-start | bytes 18436
  28.9 142.9 %copy-start.22 = (f32[1536]{0:T(1024)}, f32[1536]{0:T(1024)S(1)}, u32[]{:S(2)}) copy-start(f32[1536]{0:T(1024)S(1)} %get-tuple-element.31) | copy-start | bytes 18436
  28.9 142.9 %copy-start.23 = (f32[1536]{0:T(1024)}, f32[1536]{0:T(1024)S(1)}, u32[]{:S(2)}) copy-start(f32[1536]{0:T(1024)S(1)} %get-tuple-element.32) | copy-start | bytes 18436
  28.9 142.9 %copy-start.24 = (f32[1536]{0:T(1024)}, f32[1536]{0:T(1024)S(1)}, u32[]{:S(2)}) copy-start(f32[1536]{0:T(1024)S(1)} %get-tuple-element.33) | copy-start | bytes 18436
  28.9 142.9 %copy-start.25 = (f32[1536]{0:T(1024)}, f32[1536]{0:T(1024)S(1)}, u32[]{:S(2)}) copy-start(f32[1536]{0:T(1024)S(1)} %get-tuple-element.34) | copy-start | bytes 18436
  28.9 142.9 %copy-start.26 = (f32[1536]{0:T(1024)}, f32[1536]{0:T(1024)S(1)}, u32[]{:S(2)}) copy-start(f32[1536]{0:T(1024)S(1)} %get-tuple-element.35) | copy-start | bytes 18436
  28.9 142.9 %copy-start.27 = (f32[1536]{0:T(1024)}, f32[1536]{0:T(1024)S(1)}, u32[]{:S(2)}) copy-start(f32[1536]{0:T(1024)S(1)} %get-tuple-element.36) | copy-start | bytes 18436
  28.9 142.9 %copy-start.28 = (f32[1536]{0:T(1024)}, f32[1536]{0:T(1024)S(1)}, u32[]{:S(2)}) copy-start(f32[1536]{0:T(1024)S(1)} %get-tuple-element.37) | copy-start | bytes 18436
  29.0 142.8 %copy-start.35 = (f32[256]{0:T(256)}, f32[256]{0:T(256)S(1)}, u32[]{:S(2)}) copy-start(f32[256]{0:T(256)S(1)} %get-tuple-element.80) | copy-start | bytes 3076
  29.0 142.8 %copy-start.36 = (f32[256]{0:T(256)}, f32[256]{0:T(256)S(1)}, u32[]{:S(2)}) copy-start(f32[256]{0:T(256)S(1)} %get-tuple-element.81) | copy-start | bytes 3076
  29.0 142.8 %copy-start.37 = (f32[256]{0:T(256)}, f32[256]{0:T(256)S(1)}, u32[]{:S(2)}) copy-start(f32[256]{0:T(256)S(1)} %get-tuple-element.82) | copy-start | bytes 3076
  29.1 142.8 %copy-start.38 = (f32[256]{0:T(256)}, f32[256]{0:T(256)S(1)}, u32[]{:S(2)}) copy-start(f32[256]{0:T(256)S(1)} %get-tuple-element.53) | copy-start | bytes 3076
  29.1 142.8 %copy-start.39 = (f32[256]{0:T(256)}, f32[256]{0:T(256)S(1)}, u32[]{:S(2)}) copy-start(f32[256]{0:T(256)S(1)} %get-tuple-element.54) | copy-start | bytes 3076
  29.1 142.8 %copy-start.40 = (f32[256]{0:T(256)}, f32[256]{0:T(256)S(1)}, u32[]{:S(2)}) copy-start(f32[256]{0:T(256)S(1)} %get-tuple-element.55) | copy-start | bytes 3076
  29.1 142.8 %copy-start.41 = (f32[256]{0:T(256)}, f32[256]{0:T(256)S(1)}, u32[]{:S(2)}) copy-start(f32[256]{0:T(256)S(1)} %get-tuple-element.56) | copy-start | bytes 3076
  29.1 142.8 %copy-start.42 = (f32[256]{0:T(256)}, f32[256]{0:T(256)S(1)}, u32[]{:S(2)}) copy-start(f32[256]{0:T(256)S(1)} %get-tuple-element.57) | copy-start | bytes 3076
  29.2 142.8 %copy-start.43 = (f32[256]{0:T(256)}, f32[256]{0:T(256)S(1)}, u32[]{:S(2)}) copy-start(f32[256]{0:T(256)S(1)} %get-tuple-element.58) | copy-start | bytes 3076
  190.5 4.2 collective-permute-start.2
  193.3 6.0 %collective-permute-start.3 = (bf16[15,1536]{1,0:T(8,128)(2,1)S(1)}, bf16[15,1536]{1,0:T(8,128)(2,1)S(1)}, u32[]{:S(2)}, u32[]{:S(2)}) collective-permute-start(bf16[15,1536]{1,0:T(8,128)(2,1)S(1)} %get-tuple-element.49), channel_id=1, source_target_pairs={{8,0},{16,8},{24,16},{32,24},{40,32},{48,40},{56,48},{64,56},{72,6... | collective-permute-start | bytes 138248 | tf_op jit(solution)/shard_map/ppermute | solution.py:13
  235.7 238.1 %collective-permute-start.4 = (bf16[128,1536]{1,0:T(8,128)(2,1)S(1)}, bf16[128,1536]{1,0:T(8,128)(2,1)S(1)}, u32[]{:S(2)}, u32[]{:S(2)}) collective-permute-start(bf16[128,1536]{1,0:T(8,128)(2,1)S(1)} %get-tuple-element.47), channel_id=1, source_target_pairs={{8,0},{16,8},{24,16},{32,24},{40,32},{48,40},{56,48},{64,56},{72,6... | collective-permute-start | bytes 1179656 | tf_op jit(solution)/shard_map/ppermute | solution.py:13
  237.0 236.8 %collective-permute-start.5 = (bf16[128,1536]{1,0:T(8,128)(2,1)S(1)}, bf16[128,1536]{1,0:T(8,128)(2,1)S(1)}, u32[]{:S(2)}, u32[]{:S(2)}) collective-permute-start(bf16[128,1536]{1,0:T(8,128)(2,1)S(1)} %get-tuple-element.48), channel_id=1, source_target_pairs={{0,8},{8,16},{16,24},{24,32},{32,40},{40,48},{48,56},{56,64},{64,7... | collective-permute-start | bytes 1179656 | tf_op jit(solution)/shard_map/ppermute | solution.py:13
  469.7 8.5 %collective-permute-start.6 = (bf16[8,3072]{1,0:T(8,128)(2,1)S(1)}, bf16[8,3072]{1,0:T(8,128)(2,1)S(1)}, u32[]{:S(2)}, u32[]{:S(2)}) collective-permute-start(bf16[8,3072]{1,0:T(8,128)(2,1)S(1)} %fusion), channel_id=1, source_target_pairs={{0,1},{1,2},{2,3},{3,4},{4,5},{5,6},{6,7},{8,9},{9,10},{10,11},{11... | collective-permute-start | bytes 147464
  471.6 6.6 %collective-permute-start.7 = (bf16[6,3072]{1,0:T(8,128)(2,1)S(1)}, bf16[6,3072]{1,0:T(8,128)(2,1)S(1)}, u32[]{:S(2)}, u32[]{:S(2)}) collective-permute-start(bf16[6,3072]{1,0:T(8,128)(2,1)S(1)} %slice.684), channel_id=1, source_target_pairs={{0,2},{1,3},{2,4},{3,5},{4,6},{5,7},{8,10},{9,11},{10,12},{11,13},... | collective-permute-start | bytes 110600
  (36 other events, 2345.4 us)
Sparse Core Ops, SparseCore 0:
  24.1 106.8 all-gather.1
Sparse Core Ops, SparseCore 1:
  219.2 235.7 reduce-scatter.3
